TPU v7x, 32 devices: a whole 2x2x4 slice. The times are simulated.
32 devices in a mesh: wide: 8 (over y, x, core), narrow: 4 (over z).
Axes of the slice: x: 2, y: 2, z: 4, core: 2. Of those that a mesh axis runs over, the one named last changes fastest.
Arguments:
- inputs: bfloat16 [8, 1088, 1024], P('wide', 'narrow'), may hold values from -6 to 6
- w_qkv: bfloat16 [1024, 3072], P('narrow'), may hold values from -0.1875 to 0.1875
- w_out: bfloat16 [1024, 1024], P('narrow'), may hold values from -0.1875 to 0.1875
- w_fc1: bfloat16 [1024, 4096], P('narrow'), may hold values from -0.1875 to 0.1875
- w_fc2: bfloat16 [4096, 1024], P('narrow'), may hold values from -0.09375 to 0.09375
- norm_gain: bfloat16 [4, 1024], P(None, 'narrow'), may hold values from 0.5 to 1.5
- shifts: bfloat16 [12, 1024], P(None, 'narrow'), may hold values from -3 to 3
- text_len: int32 [8], P('wide'), may hold values from 1 to 64, as said below
- cotangent: bfloat16 [8, 1088, 1024], P('wide', 'narrow'), may hold values from -6 to 6
Outputs:
- activations: bfloat16 [8, 1088, 1024], P('wide', 'narrow')
- input_grad: bfloat16 [8, 1088, 1024], P('wide', 'narrow')
- grad_qkv: float32 [1024, 3072], P('narrow')
- grad_out: float32 [1024, 1024], P('narrow')
- grad_fc1: float32 [1024, 4096], P('narrow')
- grad_fc2: float32 [4096, 1024], P('narrow')
- grad_gain: float32 [4, 1024], P(None, 'narrow')
- grad_shift: float32 [12, 1024], P(None, 'narrow')
Inputs may be any that keep to these rules, and one draw needn't show every extreme that they name: Text positions from text_len to 63 are padding that no query reads; the first item has 64 and the last has 1.
All inputs are finite; a program needn't handle non-finite values.
Results may differ from a plain program's by a relative error of at most 0.014.
Values may be sent and summed in bfloat16 or wider, within the bound.
A program may use at most 192 MiB of HBM per device.

v0:
```python
import math

import jax
import jax.numpy as jnp
from jax import lax
from jax.sharding import PartitionSpec as P

HEADS = 16
TEXT = 64


norm_eps = 1e-05
relax_alpha = 32.0
masked_fill = -1e30


def layer_norm(values, gain, shift):
    average = jnp.mean(values, -1, keepdims=True)
    centred = values - average
    inverse = lax.rsqrt(jnp.mean(centred * centred, -1, keepdims=True) + norm_eps)
    normed = centred * inverse
    return (normed * gain + shift, normed, inverse)


def norm_back(incoming, normed, inverse, gain):
    scaled = incoming * gain
    inner_part = (
        scaled
        - jnp.mean(scaled, -1, keepdims=True)
        - normed * jnp.mean(scaled * normed, -1, keepdims=True)
    )
    return (inner_part * inverse, jnp.sum(incoming * normed, 0), jnp.sum(incoming, 0))


def left_dot(left, right):
    return lax.dot_general(
        left, right, (((0,), (0,)), ((), ())), preferred_element_type=jnp.float32
    )


def right_dot(left, right):
    return lax.dot_general(
        left, right, (((1,), (1,)), ((), ())), preferred_element_type=jnp.float32
    )


def masked_scores(queries, key_rows, allowed, head_count):
    local_rows, model_width = queries.shape
    head_size = model_width // head_count
    raw = jnp.einsum(
        "qhe,khe->hqk",
        queries.reshape(local_rows, head_count, head_size),
        key_rows.reshape(key_rows.shape[0], head_count, head_size),
        preferred_element_type=jnp.float32,
    )
    return jnp.where(allowed[None], raw * (1.0 / (relax_alpha * math.sqrt(head_size))), masked_fill)


def shards(inputs, w_qkv, w_out, w_fc1, w_fc2, norm_gain, shifts, text_len, cotangent):
    item_count, local_rows, model_width = inputs.shape
    head_count = HEADS
    head_size = model_width // head_count
    offset = lax.axis_index("narrow") * local_rows
    gathered = (
        lax.all_gather(w_qkv, "narrow", axis=0, tiled=True),
        lax.all_gather(w_out, "narrow", axis=0, tiled=True),
        lax.all_gather(w_fc1, "narrow", axis=0, tiled=True),
        lax.all_gather(w_fc2, "narrow", axis=0, tiled=True),
        lax.all_gather(norm_gain, "narrow", axis=1, tiled=True),
        lax.all_gather(shifts, "narrow", axis=1, tiled=True),
    )
    wqkv_full, wout_full, wfc1_full, wfc2_full = (
        gathered[0],
        gathered[1],
        gathered[2],
        gathered[3],
    )
    gains = gathered[4].astype(jnp.float32)
    biases = gathered[5].astype(jnp.float32)
    token_rows = inputs.reshape(item_count * local_rows, model_width).astype(jnp.float32)
    first_norm, normed_one, inverse_one = layer_norm(token_rows, gains[0], biases[0])
    first_low = first_norm.astype(jnp.bfloat16)
    joined = jnp.dot(first_low, wqkv_full, preferred_element_type=jnp.float32)
    queries = (joined[:, :model_width] + biases[4]).astype(jnp.bfloat16)
    key_rows = joined[:, model_width : 2 * model_width].astype(jnp.bfloat16)
    value_rows = (joined[:, 2 * model_width :] + biases[5]).astype(jnp.bfloat16)
    key_all, value_all = (
        lax.all_gather(
            key_rows.reshape(item_count, local_rows, model_width), "narrow", axis=1, tiled=True
        ),
        lax.all_gather(
            value_rows.reshape(item_count, local_rows, model_width), "narrow", axis=1, tiled=True
        ),
    )
    key_count = key_all.shape[1]
    query_place = offset + jnp.arange(local_rows, dtype=jnp.int32)
    key_place = jnp.arange(key_count, dtype=jnp.int32)
    member = 0
    allowed = (key_place[None, :] <= query_place[:, None]) & (
        (key_place[None, :] >= TEXT) | (key_place[None, :] < text_len[member])
    )
    scores = masked_scores(queries, key_all[member], allowed, head_count)
    row_top = jnp.max(scores, -1, keepdims=True)
    weights_exp = jnp.exp((scores - row_top) * relax_alpha)
    denom = jnp.sum(weights_exp, -1, keepdims=True)
    probs = (weights_exp / denom).astype(jnp.bfloat16)
    attended = jnp.einsum(
        "hqk,khe->qhe",
        probs,
        value_all[member].reshape(key_count, head_count, head_size),
        preferred_element_type=jnp.float32,
    )
    masks = [allowed]
    row_tops = [row_top]
    denoms = [denom]
    outputs = attended.reshape(local_rows, model_width)
    attended_low = outputs.astype(jnp.bfloat16)
    branch = jnp.dot(attended_low, wout_full, preferred_element_type=jnp.float32) + biases[6]
    branch_norm, normed_two, inverse_two = layer_norm(branch, gains[1], biases[1])
    middle = token_rows + branch_norm
    mid_norm, normed_three, inverse_three = layer_norm(middle, gains[2], biases[2])
    mid_low = mid_norm.astype(jnp.bfloat16)
    hidden = jnp.dot(mid_low, wfc1_full, preferred_element_type=jnp.float32) + biases[8:12].reshape(
        -1
    )
    active = jax.nn.gelu(hidden).astype(jnp.bfloat16)
    mlp_out = jnp.dot(active, wfc2_full, preferred_element_type=jnp.float32) + biases[7]
    mlp_norm, normed_four, inverse_four = layer_norm(mlp_out, gains[3], biases[3])
    result = middle + mlp_norm
    regathered = (
        lax.all_gather(w_qkv, "narrow", axis=0, tiled=True),
        lax.all_gather(w_out, "narrow", axis=0, tiled=True),
        lax.all_gather(w_fc1, "narrow", axis=0, tiled=True),
        lax.all_gather(w_fc2, "narrow", axis=0, tiled=True),
        lax.all_gather(norm_gain, "narrow", axis=1, tiled=True),
        lax.all_gather(shifts, "narrow", axis=1, tiled=True),
    )
    wqkv_full, wout_full, wfc1_full, wfc2_full = (
        regathered[0],
        regathered[1],
        regathered[2],
        regathered[3],
    )
    out_grad = cotangent.reshape(item_count * local_rows, model_width).astype(jnp.float32)
    d_mlp, gain_four, shift_four = norm_back(out_grad, normed_four, inverse_four, gains[3])
    d_mlp_low = d_mlp.astype(jnp.bfloat16)
    grad_fc2_term = left_dot(active, d_mlp_low)
    bias_fc2 = jnp.sum(d_mlp_low.astype(jnp.float32), 0)
    d_active = right_dot(d_mlp_low, wfc2_full)
    gelu_value, gelu_pull = jax.vjp(jax.nn.gelu, hidden)
    d_hidden = gelu_pull(d_active)[0].astype(jnp.bfloat16)
    grad_fc1_term = left_dot(mid_low, d_hidden)
    bias_fc1 = jnp.sum(d_hidden.astype(jnp.float32), 0)
    d_mid_norm = right_dot(d_hidden, wfc1_full)
    d_mid_part, gain_three, shift_three = norm_back(
        d_mid_norm, normed_three, inverse_three, gains[2]
    )
    d_middle = out_grad + d_mid_part
    d_branch, gain_two, shift_two = norm_back(d_middle, normed_two, inverse_two, gains[1])
    d_branch_low = d_branch.astype(jnp.bfloat16)
    grad_out_term = left_dot(attended_low, d_branch_low)
    bias_out = jnp.sum(d_branch_low.astype(jnp.float32), 0)
    d_attended = right_dot(d_branch_low, wout_full).astype(jnp.bfloat16)
    member = 0
    scores = masked_scores(queries, key_all[member], masks[member], head_count)
    probs = jnp.exp((scores - row_tops[member]) * relax_alpha) / denoms[member]
    probs_low = probs.astype(jnp.bfloat16)
    d_heads = d_attended.reshape(local_rows, head_count, head_size)
    key_heads = key_all[member].reshape(key_count, head_count, head_size)
    value_heads = value_all[member].reshape(key_count, head_count, head_size)
    d_probs = jnp.einsum("qhe,khe->hqk", d_heads, value_heads, preferred_element_type=jnp.float32)
    centre = jnp.sum(probs * d_probs, -1, keepdims=True)
    d_raw = (
        probs * (d_probs - centre) * (relax_alpha / (relax_alpha * math.sqrt(head_size)))
    ).astype(jnp.bfloat16)
    query_grads = jnp.einsum(
        "hqk,khe->qhe", d_raw, key_heads, preferred_element_type=jnp.float32
    ).reshape(local_rows, model_width)
    key_grads = [
        jnp.einsum(
            "hqk,qhe->khe",
            d_raw,
            queries.reshape(local_rows, head_count, head_size),
            preferred_element_type=jnp.float32,
        ).reshape(key_count, model_width)
    ]
    value_grads = [
        jnp.einsum("hqk,qhe->khe", probs_low, d_heads, preferred_element_type=jnp.float32).reshape(
            key_count, model_width
        )
    ]
    key_local, value_local = (
        lax.psum_scatter(
            jnp.stack(key_grads).astype(jnp.bfloat16), "narrow", scatter_dimension=1, tiled=True
        ).astype(jnp.float32),
        lax.psum_scatter(
            jnp.stack(value_grads).astype(jnp.bfloat16), "narrow", scatter_dimension=1, tiled=True
        ).astype(jnp.float32),
    )
    d_query_low = query_grads.astype(jnp.bfloat16)
    d_key_low = key_local.reshape(item_count * local_rows, model_width).astype(jnp.bfloat16)
    d_value_low = value_local.reshape(item_count * local_rows, model_width).astype(jnp.bfloat16)
    d_joined = jnp.concatenate([d_query_low, d_key_low, d_value_low], 1)
    grad_qkv_term = left_dot(first_low, d_joined)
    bias_query = jnp.sum(d_query_low.astype(jnp.float32), 0)
    bias_value = jnp.sum(d_value_low.astype(jnp.float32), 0)
    d_first = right_dot(d_joined, wqkv_full)
    d_input_part, gain_one, shift_one = norm_back(d_first, normed_one, inverse_one, gains[0])
    d_inputs = d_middle + d_input_part
    gain_term = jnp.stack([gain_one, gain_two, gain_three, gain_four])
    shift_term = jnp.concatenate(
        [
            jnp.stack(
                [
                    shift_one,
                    shift_two,
                    shift_three,
                    shift_four,
                    bias_query,
                    bias_value,
                    bias_out,
                    bias_fc2,
                ]
            ),
            bias_fc1.reshape(4, model_width),
        ],
        0,
    )
    pieces = (
        lax.psum_scatter(
            grad_qkv_term.astype(jnp.bfloat16), "narrow", scatter_dimension=0, tiled=True
        ).astype(jnp.float32),
        lax.psum_scatter(
            grad_out_term.astype(jnp.bfloat16), "narrow", scatter_dimension=0, tiled=True
        ).astype(jnp.float32),
        lax.psum_scatter(
            grad_fc1_term.astype(jnp.bfloat16), "narrow", scatter_dimension=0, tiled=True
        ).astype(jnp.float32),
        lax.psum_scatter(
            grad_fc2_term.astype(jnp.bfloat16), "narrow", scatter_dimension=0, tiled=True
        ).astype(jnp.float32),
        lax.psum_scatter(
            gain_term.astype(jnp.bfloat16), "narrow", scatter_dimension=1, tiled=True
        ).astype(jnp.float32),
        lax.psum_scatter(
            shift_term.astype(jnp.bfloat16), "narrow", scatter_dimension=1, tiled=True
        ).astype(jnp.float32),
    )
    summed = lax.psum((pieces[0], pieces[1], pieces[2], pieces[3], pieces[4], pieces[5]), "wide")
    activations = result.reshape(item_count, local_rows, model_width).astype(jnp.bfloat16)
    input_grad = d_inputs.reshape(item_count, local_rows, model_width).astype(jnp.bfloat16)
    return (
        activations,
        input_grad,
        summed[0],
        summed[1],
        summed[2],
        summed[3],
        summed[4],
        summed[5],
    )


def solution(mesh):
    return jax.shard_map(
        shards,
        mesh=mesh,
        in_specs=(
            P("wide", "narrow", None),
            P("narrow", None),
            P("narrow", None),
            P("narrow", None),
            P("narrow", None),
            P(None, "narrow"),
            P(None, "narrow"),
            P("wide"),
            P("wide", "narrow", None),
        ),
        out_specs=(
            P("wide", "narrow", None),
            P("wide", "narrow", None),
            P("narrow", None),
            P("narrow", None),
            P("narrow", None),
            P("narrow", None),
            P(None, "narrow"),
            P(None, "narrow"),
        ),
        check_vma=False,
    )
```

profile of v0, /device:TPU:0, one launch (start us, length us, event | category | flops | bytes accessed | tf_op | source)
XLA Modules:
  0.0 1489.5 jit_solution(17122304370244731764)
XLA Ops:
  8.0 13.7 all_gather.28
  21.6 15.0 %all_gather.29 = bf16[12,1024]{1,0:T(8,128)(2,1)S(1)} all-gather(bf16[12,256]{1,0:T(8,128)(2,1)} %param.15), channel_id=1, replica_groups=mesh['wide'=8,'narrow'=4] {'narrow'}, dimensions={1}, use_global_device_ids=true | all-gather | bytes 30720 | tf_op jit(solution)/shard_map/all_gather | solution.py:70
  36.7 1.2 convert_reduce_fusion
  38.4 89.7 %all-gather.9.cloned.1.call-done = bf16[1024,3072]{1,0:T(8,128)(2,1)} async-done(((bf16[256,3072]{1,0:T(8,128)(2,1)}), bf16[1024,3072]{1,0:T(8,128)(2,1)}) %all-gather.9.cloned.1.call-update) | async-done | bytes 6291472 | tf_op jit(solution)/shard_map/all_gather | solution.py:65
  128.0 4.8 fusion.80
  132.9 1.7 copy-done.11
  135.5 2.7 fusion.64
  141.4 40.8 %all-gather.19.cloned.1.call-done = bf16[1088,1024]{1,0:T(8,128)(2,1)} async-done(((bf16[272,1024]{1,0:T(8,128)(2,1)}), bf16[1088,1024]{1,0:T(8,128)(2,1)}) %all-gather.19.cloned.1.call-update) | async-done | bytes 2228240 | tf_op jit(solution)/shard_map/all_gather | solution.py:88
  182.3 4.1 copy.31
  186.4 45.2 %all-gather.17.cloned.1.call-done = bf16[1088,1024]{1,0:T(8,128)(2,1)} async-done(((bf16[272,1024]{1,0:T(8,128)(2,1)}), bf16[1088,1024]{1,0:T(8,128)(2,1)}) %all-gather.17.cloned.1.call-update) | async-done | bytes 2228240 | tf_op jit(solution)/shard_map/all_gather | solution.py:91
  231.6 3.0 copy.29
  234.6 13.5 exponential_reduce_fusion
  248.1 11.2 fusion.35
  259.4 18.5 %all-gather.11.cloned.1.call-done = bf16[1024,1024]{1,0:T(8,128)(2,1)} async-done(((bf16[256,1024]{1,0:T(8,128)(2,1)}), bf16[1024,1024]{1,0:T(8,128)(2,1)}) %all-gather.11.cloned.1.call-update) | async-done | bytes 2097168 | tf_op jit(solution)/shard_map/all_gather | solution.py:66
  277.8 2.8 fusion.92
  282.7 144.9 %all-gather.13.cloned.1.call-done = bf16[1024,4096]{1,0:T(8,128)(2,1)} async-done(((bf16[256,4096]{1,0:T(8,128)(2,1)}), bf16[1024,4096]{1,0:T(8,128)(2,1)}) %all-gather.13.cloned.1.call-update) | async-done | bytes 8388624 | tf_op jit(solution)/shard_map/all_gather | solution.py:67
  427.6 8.9 convolution_add_fusion
  436.6 140.4 %all-gather.15.cloned.1.call-done = bf16[4096,1024]{1,0:T(8,128)(2,1)} async-done(((bf16[1024,1024]{1,0:T(8,128)(2,1)}), bf16[4096,1024]{1,0:T(8,128)(2,1)}) %all-gather.15.cloned.1.call-update) | async-done | bytes 8388624 | tf_op jit(solution)/shard_map/all_gather | solution.py:68
  576.9 7.9 fusion.93
  585.1 1.4 fusion.63
  587.0 7.3 fusion.82
  594.4 2.9 multiply_reduce_fusion.1
  600.4 1.6 convolution_convert_fusion.4
  602.0 1.4 copy.32
  603.4 11.3 fusion.26
  614.7 11.3 copy.35
  626.0 4.5 copy.46
  630.6 8.6 fusion.97
  639.2 42.3 %fusion.29 = bf16[16,64,1088]{2,1,0:T(8,128)(2,1)S(1)} fusion(bf16[272,16,64]{0,2,1:T(8,128)(2,1)} %bitcast.156, f32[16,272,1088]{2,1,0:T(8,128)} %fusion.97, f32[16,272,1088]{2,1,0:T(8,128)} %get-tuple-element.56, f32[16,272]{1,0:T(8,128)S(1)} %copy-done.34), kind=kOutput, calls=%fused_computation.35 | convolution fusion | flops 640341312 | bytes 40682496 | tf_op jit(solution)/shard_map/hqk,qhe->khe/dot_general | solution.py:180
  681.4 8.3 copy.33
  689.7 4.6 copy.47
  694.4 3.7 convolution_convert_fusion.3
  698.3 41.9 %fusion.94 = (bf16[16,64]{1,0:T(8,128)(2,1)S(1)}, bf16[16,64,272]{2,1,0:T(8,128)(2,1)}) fusion(bf16[1088,16,64]{0,2,1:T(8,128)(2,1)S(1)} %bitcast.147, f32[16,272,1088]{2,1,0:T(8,128)} %fusion.97, f32[16,272]{1,0:T(8,128)S(1)} %copy-done.34, f32[16,272,1088]{2,1,0:T(8,128)} %get-tuple-element.56), kind=kOutput, calls=%fused_computation.145 | convolution fusion | flops 639783232 | bytes 40684544 | tf_op jit(solution)/shard_map/hqk,khe->qhe/dot_general | solution.py:176
  740.2 2.5 fusion.87
  742.7 2.2 copy.36
  744.9 1.6 reshape_bitcast_fusion.1
  746.5 2.2 copy.34
  748.7 6.6 fusion.57
  756.6 1.3 concatenate.8
  757.9 10.0 convolution_convert_fusion
  769.2 8.9 convolution_convert_fusion.1
  779.3 7.2 convolution_convert_fusion.2
  789.0 17.1 %reduce-scatter.29.cloned.1.call-done = bf16[256,4]{1,0:T(8,128)(2,1)} async-done(((bf16[1024,4]{1,0:T(8,128)(2,1)}), bf16[256,4]{1,0:T(8,128)(2,1)}) %reduce-scatter.29.cloned.1.call-update) | async-done | bytes 2064
  807.0 19.1 %reduce-scatter.23.cloned.1.call-done = bf16[12,256]{1,0:T(8,128)(2,1)} async-done(((bf16[12,1024]{1,0:T(8,128)(2,1)}), bf16[12,256]{1,0:T(8,128)(2,1)}) %reduce-scatter.23.cloned.1.call-update) | async-done | bytes 6160 | tf_op jit(solution)/shard_map/reduce_scatter | solution.py:245
  826.1 145.0 %reduce-scatter.21.cloned.1.call-done = bf16[1024,1024]{1,0:T(8,128)(2,1)} async-done(((bf16[4096,1024]{1,0:T(8,128)(2,1)}), bf16[1024,1024]{1,0:T(8,128)(2,1)}) %reduce-scatter.21.cloned.1.call-update) | async-done | bytes 2097168 | tf_op jit(solution)/shard_map/reduce_scatter | solution.py:239
  971.1 147.7 %reduce-scatter.19.cloned.1.call-done = bf16[256,4096]{1,0:T(8,128)(2,1)} async-done(((bf16[1024,4096]{1,0:T(8,128)(2,1)}), bf16[256,4096]{1,0:T(8,128)(2,1)}) %reduce-scatter.19.cloned.1.call-update) | async-done | bytes 2097168 | tf_op jit(solution)/shard_map/reduce_scatter | solution.py:236
  1118.8 113.8 %reduce-scatter.15.cloned.1.call-done = bf16[256,3072]{1,0:T(8,128)(2,1)} async-done(((bf16[1024,3072]{1,0:T(8,128)(2,1)}), bf16[256,3072]{1,0:T(8,128)(2,1)}) %reduce-scatter.15.cloned.1.call-update) | async-done | bytes 1572880 | tf_op jit(solution)/shard_map/reduce_scatter | solution.py:230
  1232.5 250.0 %all-reduce.2 = (f32[256,3072]{1,0:T(8,128)}, f32[256,1024]{1,0:T(8,128)}, f32[256,4096]{1,0:T(8,128)}, f32[1024,1024]{1,0:T(8,128)}, f32[4,256]{1,0:T(4,128)}, /*index=5*/f32[12,256]{1,0:T(8,128)}) all-reduce(bf16[256,3072]{1,0:T(8,128)(2,1)} %reduce-scatter.15.cloned.1.call-done, ...), channel_id=1, replica_groups=mesh['wide'=8,'narrow'=4] {'wide'}, use_global_device_ids=true, to_apply=%region_22.23 | all-reduce | flops 3149824 | bytes 18898944 | tf_op jit(solution)/shard_map/psum | solution.py:249
  (156 shorter events, 17.6 us)
Async XLA Ops:
  7.2 30.8 %copy-start.5 = (bf16[1,272,1024]{2,1,0:T(8,128)(2,1)S(1)}, bf16[1,272,1024]{2,1,0:T(8,128)(2,1)}, u32[]{:S(2)}) copy-start(bf16[1,272,1024]{2,1,0:T(8,128)(2,1)} %param.9) | copy-start | bytes 1671172
  7.2 120.8 %all-gather.9.cloned.1.call-start = ((), (), s32[]{:S(2)}) async-start(), calls=%async_computation.8 | async-start | bytes 7864320 | tf_op jit(solution)/shard_map/all_gather | solution.py:65
  7.9 174.3 %all-gather.19.cloned.1.call-start = ((), (), s32[]{:S(2)}) async-start(), calls=%async_computation.18 | async-start | bytes 2785280 | tf_op jit(solution)/shard_map/all_gather | solution.py:88
  37.9 94.9 %copy-start.21 = (f32[272]{0:T(512)}, f32[272]{0:T(512)S(1)}, u32[]{:S(2)}) copy-start(f32[272]{0:T(512)S(1)} %broadcast_multiply_fusion.11) | copy-start | bytes 3268
  38.3 94.6 %copy-start.25 = (f32[272]{0:T(512)}, f32[272]{0:T(512)S(1)}, u32[]{:S(2)}) copy-start(f32[272]{0:T(512)S(1)} %add_rsqrt_fusion.3) | copy-start | bytes 3268
  38.3 94.5 %copy-start.23 = (f32[1,1024]{1,0:T(1,128)}, f32[1,1024]{1,0:T(1,128)S(1)}, u32[]{:S(2)}) copy-start(f32[1,1024]{1,0:T(1,128)S(1)} %get-tuple-element.54) | copy-start | bytes 12292
  38.3 94.5 %copy-start.27 = (f32[1,1024]{1,0:T(1,128)}, f32[1,1024]{1,0:T(1,128)S(1)}, u32[]{:S(2)}) copy-start(f32[1,1024]{1,0:T(1,128)S(1)} %get-tuple-element.50) | copy-start | bytes 12292
  38.4 389.3 %copy-start.29 = (f32[1,1024]{1,0:T(1,128)}, f32[1,1024]{1,0:T(1,128)S(1)}, u32[]{:S(2)}) copy-start(f32[1,1024]{1,0:T(1,128)S(1)} %get-tuple-element.44) | copy-start | bytes 12292
  132.9 1.7 copy-start.11
  135.5 96.1 %all-gather.17.cloned.1.call-start = ((), (), s32[]{:S(2)}) async-start(), calls=%async_computation.17 | async-start | bytes 2785280 | tf_op jit(solution)/shard_map/all_gather | solution.py:91
  138.2 139.6 %all-gather.11.cloned.1.call-start = ((), (), s32[]{:S(2)}) async-start(), calls=%async_computation.9 | async-start | bytes 2621440 | tf_op jit(solution)/shard_map/all_gather | solution.py:66
  138.8 288.8 %all-gather.13.cloned.1.call-start = ((), (), s32[]{:S(2)}) async-start(), calls=%async_computation.10 | async-start | bytes 10485760 | tf_op jit(solution)/shard_map/all_gather | solution.py:67
  139.4 437.5 %all-gather.15.cloned.1.call-start = ((), (), s32[]{:S(2)}) async-start(), calls=%async_computation.11 | async-start | bytes 10485760 | tf_op jit(solution)/shard_map/all_gather | solution.py:68
  140.0 600.2 %reduce-scatter.27.cloned.1.call-start = ((), (), s32[]{:S(2)}) async-start(), calls=%async_computation.20 | async-start | bytes 2785280
  141.0 107.1 %copy-start.20 = (pred[272,1088]{1,0:T(8,128)(4,1)}, pred[272,1088]{1,0:T(8,128)(4,1)S(1)}, u32[]{:S(2)}) copy-start(pred[272,1088]{1,0:T(8,128)(4,1)S(1)} %fusion.49) | copy-start | bytes 887812
  141.4 106.7 %copy-start.14 = (bf16[272,1024]{0,1:T(8,128)(2,1)}, bf16[272,1024]{0,1:T(8,128)(2,1)S(1)}, u32[]{:S(2)}) copy-start(bf16[272,1024]{0,1:T(8,128)(2,1)S(1)} %copy.30) | copy-start | bytes 1671172
  248.1 11.3 copy-start.33
  277.8 3.1 copy-start.6
  576.9 8.2 copy-start.1
  576.9 8.2 copy-start.8
  576.9 10.0 copy-start.31
  586.6 7.8 slice-start
  587.0 7.4 copy-start.16
  587.0 7.4 slice-start.1
  594.4 2.9 copy-start.32
  598.4 2.0 copy-start.12
  600.4 3.0 copy-start.34
  630.5 114.3 %reduce-scatter.25.cloned.1.call-start = ((), (), s32[]{:S(2)}) async-start(), calls=%async_computation.19 | async-start | bytes 2785280
  689.7 4.7 copy-start.13
  694.3 3.9 copy-start.10
  694.3 92.2 %reduce-scatter.17.cloned.1.call-start = ((), (), s32[]{:S(2)}) async-start(), calls=%async_computation.13 | async-start | bytes 2621440 | tf_op jit(solution)/shard_map/reduce_scatter | solution.py:233
  698.2 107.9 %reduce-scatter.29.cloned.1.call-start = ((), (), s32[]{:S(2)}) async-start(), calls=%async_computation.21 | async-start | bytes 327680
  742.6 6.0 copy-start.7
  742.6 6.0 copy-start.22
  742.7 6.0 copy-start.24
  742.7 6.0 copy-start.26
  748.7 7.6 copy-start.9
  748.7 9.3 copy-start.17
  756.2 69.9 %reduce-scatter.23.cloned.1.call-start = ((), (), s32[]{:S(2)}) async-start(), calls=%async_computation.16 | async-start | bytes 40960 | tf_op jit(solution)/shard_map/reduce_scatter | solution.py:245
  757.9 213.2 %reduce-scatter.21.cloned.1.call-start = ((), (), s32[]{:S(2)}) async-start(), calls=%async_computation.15 | async-start | bytes 10485760 | tf_op jit(solution)/shard_map/reduce_scatter | solution.py:239
  768.0 1.2 copy-start.2
  768.0 1.2 copy-start.30
  768.0 350.8 %reduce-scatter.19.cloned.1.call-start = ((), (), s32[]{:S(2)}) async-start(), calls=%async_computation.14 | async-start | bytes 10485760 | tf_op jit(solution)/shard_map/reduce_scatter | solution.py:236
  778.1 1.1 copy-start.15
  778.1 1.1 copy-start.28
  778.2 454.4 %reduce-scatter.15.cloned.1.call-start = ((), (), s32[]{:S(2)}) async-start(), calls=%async_computation.12 | async-start | bytes 7864320 | tf_op jit(solution)/shard_map/reduce_scatter | solution.py:230
  786.5 1.2 copy-start.4
  786.6 446.0 %copy-start.19 = (bf16[256,1024]{1,0:T(8,128)(2,1)S(1)}, bf16[256,1024]{1,0:T(8,128)(2,1)}, u32[]{:S(2)}) copy-start(bf16[256,1024]{1,0:T(8,128)(2,1)} %reduce-scatter.17.cloned.1.call-done) | copy-start | bytes 1572868
  (3 other events, 2.8 us)
Sparse Core Ops, SparseCore 0:
  9.6 118.3 all-gather.8
  135.6 46.6 all-gather.18
  184.4 47.1 all-gather.16
  233.0 44.7 all-gather.10
  279.2 148.3 all-gather.12
  429.0 147.8 all-gather.14
  630.6 44.1 reduce-scatter.26
  694.4 44.2 reduce-scatter.24
  741.0 43.2 reduce-scatter.16
  787.1 18.9 reduce-scatter.28
  808.9 17.1 reduce-scatter.22
  828.5 142.5 reduce-scatter.20
  973.6 145.1 reduce-scatter.18
  1121.0 111.4 reduce-scatter.14
where the time goes:
time: 1500 us; the launch traced here: 1490 us
  waiting for transfers between devices  925 us (62%)
  blocking collectives  279 us (19%)
  matrix products  201 us (13%)
  local copies, waits for them, and re-layouts  55.5 us (4%)
  between operations  15.7 us (1%)
    psum x1, blocking collectives, shards(): lax.psum((pieces[0], pieces[1], pieces[2], pieces[3], pieces[4], pieces[5...  250 us
    reduce_scatter x1, waiting for transfers between devices, shards(): lax.psum_scatter(grad_fc1_term.astype(jnp.bfloat16), 'narrow', scatter_di...  148 us
    reduce_scatter x1, waiting for transfers between devices, shards(): lax.psum_scatter(grad_fc2_term.astype(jnp.bfloat16), 'narrow', scatter_di...  145 us
    all_gather x1, waiting for transfers between devices, shards(): lax.all_gather(w_fc1, 'narrow', axis=0, tiled=True)  145 us
    all_gather x1, waiting for transfers between devices, shards(): lax.all_gather(w_fc2, 'narrow', axis=0, tiled=True)  140 us
    reduce_scatter x1, waiting for transfers between devices, shards(): lax.psum_scatter(grad_qkv_term.astype(jnp.bfloat16), 'narrow', scatter_di...  114 us
    all_gather x1, waiting for transfers between devices, shards(): lax.all_gather(w_qkv, 'narrow', axis=0, tiled=True)  89.7 us
    all_gather x1, waiting for transfers between devices, shards(): lax.all_gather(value_rows.reshape(item_count, local_rows, model_width), '...  45.2 us
  transfers between devices with their start and end apart: 14, of which 11 were waited for; matrix products, arithmetic and copies ran while one was open for 14% of the time, Pallas kernels for 0%

commit v1 on v0

v1 whole, which is shorter than its diff:
```python
import functools
import math

import jax
import jax.numpy as jnp
from jax import lax
from jax.experimental import pallas as pl
from jax.experimental.pallas import tpu as pltpu
from jax.sharding import PartitionSpec as P

HEADS = 16
TEXT = 64
EPS = 1e-5
GROUP = 8
MESH = pl.DeviceIdType.MESH
F32 = jnp.float32
BF16 = jnp.bfloat16
ANY = pl.BlockSpec(memory_space=pl.ANY)
VMEM = pl.BlockSpec(memory_space=pltpu.VMEM)
SMEM = pl.BlockSpec(memory_space=pltpu.SMEM)
DMA = pltpu.SemaphoreType.DMA


def at(start, size, step=16):
    return pl.ds(pl.multiple_of(start, step), size)


def place():
    w = lax.axis_index("wide")
    z = lax.axis_index("narrow")
    return w, z, lax.rem(w, 2), lax.rem(lax.div(w, 2), 2), lax.rem(lax.div(w, 4), 2)


def flips(w, core, x, y, j):
    return (
        w
        + (j & 1) * (1 - 2 * core)
        + ((j >> 1) & 1) * (2 - 4 * x)
        + ((j >> 2) & 1) * (4 - 8 * y)
    )


def remote(src, dst, send_sem, recv_sem, device):
    return pltpu.make_async_remote_copy(
        src_ref=src,
        dst_ref=dst,
        send_sem=send_sem,
        recv_sem=recv_sem,
        device_id=device,
        device_id_type=MESH,
    )


def meet(devices):
    barrier = pltpu.get_barrier_semaphore()
    for device in devices:
        pl.semaphore_signal(barrier, inc=1, device_id=device, device_id_type=MESH)
    pl.semaphore_wait(barrier, len(devices))


def dot(left, right):
    return lax.dot_general(left, right, (((1,), (0,)), ((), ())), preferred_element_type=F32)


def dot_nt(left, right):
    return lax.dot_general(left, right, (((1,), (1,)), ((), ())), preferred_element_type=F32)


def dot_tn(left, right):
    return lax.dot_general(left, right, (((0,), (0,)), ((), ())), preferred_element_type=F32)


def norm(values):
    centred = values - jnp.mean(values, -1, keepdims=True)
    inverse = lax.rsqrt(jnp.mean(centred * centred, -1, keepdims=True) + EPS)
    return centred * inverse, inverse


def norm_back(incoming, normed, inverse, gain):
    scaled = incoming * gain
    return inverse * (
        scaled
        - jnp.mean(scaled, -1, keepdims=True)
        - normed * jnp.mean(scaled * normed, -1, keepdims=True)
    )


def rowsum(values):
    return jnp.sum(values, 0, keepdims=True)


def lanes(rows, width, head):
    lane = lax.broadcasted_iota(jnp.int32, (rows, width), 1)
    size = width // 4
    return ((lane >= head * size) & (lane < head * size + size)).astype(F32)


def widths(rows, blocks):
    return [-(-rows * (b + 1) // 128) * 128 for b in range(blocks)]


def attend_kernel(
    NZ,
    x_ref,
    par_ref,
    len_ref,
    wqkv_ref,
    wout_ref,
    wfc1_ref,
    wfc2_ref,
    o4_out,
    h1_out,
    q_out,
    k_out,
    v_out,
    wq_out,
    a_out,
    b_out,
    wo_out,
    par_out,
    p_out,
    par_all,
    par_f,
    stage,
    wq,
    a_ref,
    b_ref,
    wo_ref,
    h1,
    q_s,
    k_s,
    v_s,
    mask_s,
    p_s,
    o_acc,
    o_send,
    o4,
    loc_sem,
    par_s,
    par_r,
    wz_s,
    wz_r,
    wp_s,
    wp_r,
    up_s,
    up_r,
    dn_s,
    dn_r,
    fz_s,
    fz_r,
    fp_s,
    fp_r,
    sib_s,
    sib_r,
    o_s,
    o_r,
    out_sem,
):
    R, D = x_ref.shape
    C = D // NZ
    FH = wfc1_ref.shape[1] // (2 * NZ)
    w, z, core, x, y = place()
    chip = x + 2 * y
    w8 = core + 2 * chip
    near = {j: flips(w, core, x, y, j) for j in range(1, GROUP)}
    zto = [lax.rem(z + j, NZ) for j in range(NZ)]
    zfrom = [lax.rem(z + NZ - j, NZ) for j in range(NZ)]
    hops = range(1, NZ)
    pending = []

    meet([(w, zto[j]) for j in hops] + [(near[j], z) for j in range(1, GROUP)])

    def go(copy):
        copy.start()
        pending.append(copy)

    for j in hops:
        go(remote(par_ref, par_all.at[z], par_s.at[j], par_r.at[j], (w, zto[j])))
    own_par = pltpu.make_async_copy(par_ref, par_all.at[z], loc_sem.at[0])
    own_par.start()

    staged = []
    for d in range(NZ):
        for t in range(3):
            copy = pltpu.make_async_copy(
                wqkv_ref.at[:, pl.ds(t * D + d * C, C)],
                stage.at[d, :, pl.ds(t * C, C)],
                loc_sem.at[1 + 3 * d + t],
            )
            copy.start()
            staged.append(copy)
    local = 1 + 3 * NZ
    owned = []
    for j in range(NZ):
        owned.append(
            pltpu.make_async_copy(
                wfc1_ref.at[:, at((2 * j) * FH + core * FH, FH, 128)],
                a_ref.at[at(z * C, C), pl.ds(j * FH, FH)],
                loc_sem.at[local + j],
            )
        )
    owned.append(
        pltpu.make_async_copy(
            wfc2_ref.at[at(core * FH, FH)], b_ref.at[z], loc_sem.at[local + NZ]
        )
    )
    owned.append(
        pltpu.make_async_copy(wout_ref, wo_ref.at[at(z * C, C)], loc_sem.at[local + NZ + 1])
    )
    for copy in owned:
        copy.start()

    normed, _ = norm(x_ref[...].astype(F32))
    for copy in staged:
        copy.wait()
    RW = C // GROUP
    for j in hops:
        go(
            remote(
                stage.at[zto[j], at(w8 * RW, RW)],
                wq.at[at(z * C + w8 * RW, RW)],
                wz_s.at[j],
                wz_r.at[j],
                (w, zto[j]),
            )
        )
    own_wq = pltpu.make_async_copy(stage.at[z], wq.at[at(z * C, C)], loc_sem.at[local + NZ + 2])
    own_wq.start()
    own_par.wait()
    for j in hops:
        remote(
            par_ref, par_all.at[zfrom[j]], par_s.at[j], par_r.at[j], (w, zto[j])
        ).wait_recv()
    for d in range(NZ):
        par_f[:, d * C : (d + 1) * C] = par_all[d].astype(F32)
    h1[at(z * R, R), :] = (normed * par_f[0:1, :] + par_f[4:5, :]).astype(BF16)

    def upward(k):
        block = h1.at[at(jnp.maximum(z - k, 0) * R, R)]
        return remote(block, block, up_s.at[k], up_r.at[k], (w, jnp.minimum(z + 1, NZ - 1)))

    def downward(k):
        block = h1.at[at(jnp.minimum(z + k, NZ - 1) * R, R)]
        return remote(block, block, dn_s.at[k], dn_r.at[k], (w, jnp.maximum(z - 1, 0)))

    def from_below(k):
        block = h1.at[at(jnp.maximum(z - 1 - k, 0) * R, R)]
        return remote(block, block, up_s.at[k], up_r.at[k], (w, jnp.minimum(z + 1, NZ - 1)))

    def from_above(k):
        block = h1.at[at(jnp.minimum(z + 1 + k, NZ - 1) * R, R)]
        return remote(block, block, dn_s.at[k], dn_r.at[k], (w, jnp.maximum(z - 1, 0)))

    def relay(k):
        up, down = upward(k), downward(k)

        @pl.when((z - k >= 0) & (z < NZ - 1))
        def _():
            up.start()

        @pl.when((z + k <= NZ - 1) & (z > 0))
        def _():
            down.start()

    relay(0)

    def piece(kind, source, quarter):
        if kind == 0:
            n = C // 4
            return a_ref.at[at(source * C + quarter * n, n)]
        if kind == 1:
            n = FH // 4
            return b_ref.at[source, at(quarter * n, n)]
        n = C // 8
        return wo_ref.at[at(source * C + core * (C // 2) + quarter * n, n)]

    def fetch(kind):
        for j in hops:
            part = piece(kind, z, chip)
            go(remote(part, part, fz_s.at[kind, j], fz_r.at[kind, j], (w, zto[j])))

    def spread(kind):
        for j in hops:
            part = piece(kind, zfrom[j], chip)
            remote(part, part, fz_s.at[kind, j], fz_r.at[kind, j], (w, zto[j])).wait_recv()
            for t in range(1, 4):
                go(
                    remote(
                        part,
                        part,
                        fp_s.at[kind, j, t],
                        fp_r.at[kind, j, t],
                        (near[2 * t], z),
                    )
                )

    def gathered(kind):
        for j in hops:
            for t in range(1, 4):
                other = (x + (t & 1) * (1 - 2 * x)) + 2 * (y + (t >> 1) * (1 - 2 * y))
                part = piece(kind, zfrom[j], other)
                remote(
                    part, part, fp_s.at[kind, j, t], fp_r.at[kind, j, t], (near[2 * t], z)
                ).wait_recv()

    for copy in owned:
        copy.wait()
    fetch(0)

    for j in hops:
        part = wq.at[at(zfrom[j] * C + w8 * RW, RW)]
        remote(part, part, wz_s.at[j], wz_r.at[j], (w, zto[j])).wait_recv()
        for t in range(1, GROUP):
            go(remote(part, part, wp_s.at[j, t], wp_r.at[j, t], (near[t], z)))
    own_wq.wait()
    for j in hops:
        for t in range(1, GROUP):
            other = near[t] - w + w8
            part = wq.at[at(zfrom[j] * C + other * RW, RW)]
            remote(part, part, wp_s.at[j, t], wp_r.at[j, t], (near[t], z)).wait_recv()

    rows_k = k_s.shape[0]
    total = NZ * R
    if rows_k > total:
        k_s[total:rows_k, :] = jnp.zeros((rows_k - total, C), BF16)
        v_s[total:rows_k, :] = jnp.zeros((rows_k - total, C), BF16)
    bias_q = par_ref[...].astype(F32)[8:9, :]
    bias_v = par_ref[...].astype(F32)[9:10, :]

    def project(block):
        rows = at(block * R, R)
        q_s[rows, :] = (dot(h1[rows, :], wq[:, 0:C]) + bias_q).astype(BF16)
        k_s[rows, :] = dot(h1[rows, :], wq[:, C : 2 * C]).astype(BF16)
        v_s[rows, :] = (dot(h1[rows, :], wq[:, 2 * C : 3 * C]) + bias_v).astype(BF16)

    project(z)
    for k in range(NZ - 1):
        below, above = from_below(k), from_above(k)

        @pl.when(z - 1 - k >= 0)
        def _():
            below.wait_recv()

        @pl.when(z + 1 + k <= NZ - 1)
        def _():
            above.wait_recv()

        if k + 1 < NZ - 1:
            relay(k + 1)
        if k == 0:
            fetch(1)
            fetch(2)
        if k == 1:
            spread(0)

        @pl.when(z - 1 - k >= 0)
        def _():
            project(z - 1 - k)

        @pl.when(z + 1 + k <= NZ - 1)
        def _():
            project(z + 1 + k)

    outs = []

    def emit(src, dst, sem):
        copy = pltpu.make_async_copy(src, dst, out_sem.at[sem])
        copy.start()
        outs.append(copy)

    emit(h1, h1_out, 0)
    emit(q_s, q_out, 1)
    emit(k_s, k_out, 2)
    emit(v_s, v_out, 3)
    emit(wq, wq_out, 4)
    emit(par_f, par_out, 5)
    spread(1)
    spread(2)

    scale = math.log2(math.e) / math.sqrt(C // 4)
    text_len = len_ref[0]
    for b, width in enumerate(widths(R, NZ)):
        row = lax.broadcasted_iota(jnp.int32, (R, width), 0) + b * R
        col = lax.broadcasted_iota(jnp.int32, (R, width), 1)
        allowed = (col <= row) & ((col >= TEXT) | (col < text_len))
        mask_s[:, :width] = jnp.where(allowed, 0.0, -1e30)
        o_acc[...] = jnp.zeros_like(o_acc)

        @pl.loop(0, 4)
        def _(h):
            pick = lanes(R, C, h)
            q_h = q_s[b * R : (b + 1) * R, :] * pick.astype(BF16)
            s = dot_nt(q_h, k_s[:width, :]) + mask_s[:, :width]
            e = jnp.exp2((s - jnp.max(s, -1, keepdims=True)) * scale)
            p = (e * (1.0 / jnp.sum(e, -1, keepdims=True))).astype(BF16)
            p_s[b, at(h * R, R), :width] = p
            o_acc[...] += dot(p, v_s[:width, :]) * pick

        emit(p_s.at[b, :, pl.ds(0, width)], p_out.at[b, :, pl.ds(0, width)], 6 + b)
        o_send[b * R : (b + 1) * R, :] = o_acc[...].astype(BF16)
        send = remote(
            o_send.at[pl.ds(b * R, R)], o4.at[z], o_s.at[b], o_r.at[z], (w, jnp.int32(b))
        )

        @pl.when(z != b)
        def _():
            send.start()

        @pl.when(z == b)
        def _():
            o4[z] = o_send[b * R : (b + 1) * R, :]

    for kind in range(3):
        gathered(kind)
    for j in hops:
        part = wo_ref.at[at(zfrom[j] * C + core * (C // 2), C // 2)]
        go(remote(part, part, sib_s.at[j], sib_r.at[j], (near[1], z)))
    for d in range(NZ):
        send = remote(
            o_send.at[pl.ds(d * R, R)], o4.at[d], o_s.at[d], o_r.at[d], (w, jnp.int32(d))
        )

        @pl.when(z != d)
        def _():
            send.wait_send()
            send.wait_recv()

    emit(o4, o4_out, 6 + NZ)
    emit(a_ref, a_out, 7 + NZ)
    emit(b_ref, b_out, 8 + NZ)
    for j in hops:
        part = wo_ref.at[at(zfrom[j] * C + (1 - core) * (C // 2), C // 2)]
        remote(part, part, sib_s.at[j], sib_r.at[j], (near[1], z)).wait_recv()
    emit(wo_ref, wo_out, 9 + NZ)
    for k in range(NZ - 1):
        up, down = upward(k), downward(k)

        @pl.when((z - k >= 0) & (z < NZ - 1))
        def _():
            up.wait_send()

        @pl.when((z + k <= NZ - 1) & (z > 0))
        def _():
            down.wait_send()

    for copy in pending:
        copy.wait_send()
    for copy in outs:
        copy.wait()


def attend(NZ, inputs, par, text_len, w_qkv, w_out, w_fc1, w_fc2):
    R, D = inputs.shape
    C = D // NZ
    FH = w_fc1.shape[1] // (2 * NZ)
    T = NZ * R
    wide = widths(R, NZ)[-1]
    shape = jax.ShapeDtypeStruct
    return pl.pallas_call(
        functools.partial(attend_kernel, NZ),
        out_shape=[
            shape((NZ, R, C), BF16),
            shape((T, D), BF16),
            shape((T, C), BF16),
            shape((wide, C), BF16),
            shape((wide, C), BF16),
            shape((D, 3 * C), BF16),
            shape((D, NZ * FH), BF16),
            shape((NZ, FH, D), BF16),
            shape((D, D), BF16),
            shape((16, D), F32),
            shape((NZ, 4 * R, wide), BF16),
        ],
        in_specs=[VMEM, VMEM, SMEM, ANY, ANY, ANY, ANY],
        out_specs=[ANY] * 11,
        scratch_shapes=[
            pltpu.VMEM((NZ, 16, C), BF16),
            pltpu.VMEM((16, D), F32),
            pltpu.VMEM((NZ, C, 3 * C), BF16),
            pltpu.VMEM((D, 3 * C), BF16),
            pltpu.VMEM((D, NZ * FH), BF16),
            pltpu.VMEM((NZ, FH, D), BF16),
            pltpu.VMEM((D, D), BF16),
            pltpu.VMEM((T, D), BF16),
            pltpu.VMEM((T, C), BF16),
            pltpu.VMEM((wide, C), BF16),
            pltpu.VMEM((wide, C), BF16),
            pltpu.VMEM((R, wide), F32),
            pltpu.VMEM((NZ, 4 * R, wide), BF16),
            pltpu.VMEM((R, C), F32),
            pltpu.VMEM((T, C), BF16),
            pltpu.VMEM((NZ, R, C), BF16),
            DMA((4 * NZ + 4,)),
            DMA((NZ,)),
            DMA((NZ,)),
            DMA((NZ,)),
            DMA((NZ,)),
            DMA((NZ, GROUP)),
            DMA((NZ, GROUP)),
            DMA((NZ,)),
            DMA((NZ,)),
            DMA((NZ,)),
            DMA((NZ,)),
            DMA((3, NZ)),
            DMA((3, NZ)),
            DMA((3, NZ, 4)),
            DMA((3, NZ, 4)),
            DMA((NZ,)),
            DMA((NZ,)),
            DMA((NZ,)),
            DMA((NZ,)),
            DMA((10 + NZ,)),
        ],
        compiler_params=pltpu.CompilerParams(
            collective_id=0, has_side_effects=True, vmem_limit_bytes=56 * 2**20
        ),
    )(inputs, par, text_len, w_qkv, w_out, w_fc1, w_fc2)


def feed_kernel(
    NZ,
    x_ref,
    cot_ref,
    o4_ref,
    par_ref,
    a_hbm,
    b_hbm,
    wo_hbm,
    act_ref,
    dmid_ref,
    do_ref,
    ga_out,
    gb_out,
    go_out,
    small_ref,
    wa,
    wb,
    wo,
    h3,
    gate,
    slope,
    dm,
    du,
    part,
    far_m,
    far_h,
    mid_s,
    n2_s,
    n3_s,
    ga,
    gb,
    go_s,
    load_sem,
    send_sem,
    recv_sem,
    out_sem,
):
    R, D = x_ref.shape
    C = D // NZ
    FH = b_hbm.shape[1]
    w, z, core, x, y = place()
    other = (flips(w, core, x, y, 1), z)
    loads = [
        pltpu.make_async_copy(src, dst, load_sem.at[i])
        for i, (src, dst) in enumerate(((wo_hbm, wo), (a_hbm, wa), (b_hbm, wb)))
    ]
    for copy in loads:
        copy.start()
    meet([other])
    swaps = []

    def swap(src, dst, i):
        copy = remote(src, dst, send_sem.at[i], recv_sem.at[i], other)
        copy.start()
        swaps.append(copy)
        return copy

    def param(row):
        return par_ref[row : row + 1, :]

    shift = 4
    mine, theirs = slice(0, R), slice(R, 2 * R)

    loads[0].wait()
    branch = dot(o4_ref[0], wo[0:C, :])
    for s in range(1, NZ):
        branch += dot(o4_ref[s], wo[s * C : (s + 1) * C, :])
    n2, r2 = norm(branch + param(shift + 6))
    mid = x_ref[...].astype(F32) + n2 * param(1) + param(shift + 1)
    n2_s[...] = n2
    mid_s[...] = mid
    n3, r3 = norm(mid)
    n3_s[...] = n3
    h3[mine, :] = (n3 * param(2) + param(shift + 2)).astype(BF16)
    swap_h = swap(h3.at[pl.ds(0, R)], h3.at[pl.ds(R, R)], 0)
    loads[1].wait()

    def hidden(rows):
        for s in range(NZ):
            cols = slice(s * FH, (s + 1) * FH)
            line = par_ref[shift + 8 + s : shift + 9 + s, :]
            bias = jnp.where(core == 0, line[:, :FH], line[:, FH:])
            u = dot(h3[rows, :], wa[:, cols]) + bias
            k = math.sqrt(2.0 / math.pi)
            sq = u * u
            t = jnp.tanh(u * (k + k * 0.044715 * sq))
            half = 0.5 + 0.5 * t
            gate[rows, cols] = (u * half).astype(BF16)
            slope[rows, cols] = (
                half + (0.5 * u) * (1.0 - t * t) * (k + 3.0 * k * 0.044715 * sq)
            ).astype(BF16)

    def contract(rows):
        total = dot(gate[rows, 0:FH], wb[0])
        for s in range(1, NZ):
            total += dot(gate[rows, s * FH : (s + 1) * FH], wb[s])
        return total

    hidden(mine)
    loads[2].wait()
    swap_h.wait_recv()
    hidden(theirs)
    part[0] = contract(theirs).astype(BF16)
    swap_m = swap(part.at[0], far_m, 1)
    m_near = contract(mine)
    swap_m.wait_recv()
    n4, r4 = norm(m_near + far_m[...].astype(F32) + param(shift + 7))
    act_ref[...] = (mid_s[...] + n4 * param(3) + param(shift + 3)).astype(BF16)

    e = cot_ref[...].astype(F32)
    small_ref[...] = jnp.zeros_like(small_ref)
    small_ref[3:4, :] = rowsum(e * n4)
    small_ref[shift + 3 : shift + 4, :] = rowsum(e)
    dm_low = norm_back(e, n4, r4, param(3)).astype(BF16)
    dm[mine, :] = dm_low
    small_ref[shift + 7 : shift + 8, :] = rowsum(dm_low.astype(F32))
    swap_d = swap(dm.at[pl.ds(0, R)], dm.at[pl.ds(R, R)], 2)

    def unhidden(rows):
        for s in range(NZ):
            cols = slice(s * FH, (s + 1) * FH)
            du[rows, cols] = (
                dot_nt(dm[rows, :], wb[s]) * slope[rows, cols].astype(F32)
            ).astype(BF16)

    unhidden(mine)
    swap_d.wait_recv()
    unhidden(theirs)
    part[1] = dot_nt(du[theirs, :], wa[...]).astype(BF16)
    swap_u = swap(part.at[1], far_h, 3)
    outs = []

    def emit(src, dst, i):
        copy = pltpu.make_async_copy(src, dst, out_sem.at[i])
        copy.start()
        outs.append(copy)

    for s in range(NZ):
        cols = slice(s * FH, (s + 1) * FH)
        gb[s] = dot_tn(gate[:, cols], dm[...]).astype(BF16)
    emit(gb, gb_out, 0)
    for s in range(NZ):
        cols = slice(s * FH, (s + 1) * FH)
        ga[:, cols] = dot_tn(h3[...], du[:, cols]).astype(BF16)
        total = rowsum(du[:, cols].astype(F32))
        row = shift + 8 + s
        small_ref[row : row + 1, 0:FH] = jnp.where(core == 0, total, 0.0)
        small_ref[row : row + 1, FH:] = jnp.where(core == 0, 0.0, total)
    emit(ga, ga_out, 1)
    dh3 = dot_nt(du[mine, :], wa[...])
    swap_u.wait_recv()
    dh3 += far_h[...].astype(F32)
    n3 = n3_s[...]
    small_ref[2:3, :] = rowsum(dh3 * n3)
    small_ref[shift + 2 : shift + 3, :] = rowsum(dh3)
    dmid = e + norm_back(dh3, n3, r3, param(2))
    dmid_ref[...] = dmid
    n2 = n2_s[...]
    small_ref[1:2, :] = rowsum(dmid * n2)
    small_ref[shift + 1 : shift + 2, :] = rowsum(dmid)
    da = norm_back(dmid, n2, r2, param(1)).astype(BF16)
    small_ref[shift + 6 : shift + 7, :] = rowsum(da.astype(F32))
    for s in range(NZ):
        do_ref[s] = dot_nt(da, wo[s * C : (s + 1) * C, :]).astype(BF16)
        go_s[s] = dot_tn(o4_ref[s], da).astype(BF16)
    emit(go_s, go_out, 2)
    for copy in swaps:
        copy.wait_send()
    for copy in outs:
        copy.wait()


def feed(NZ, inputs, cotangent, o4, par, wa, wb, wo):
    R, D = inputs.shape
    C = D // NZ
    FH = wb.shape[1]
    shape = jax.ShapeDtypeStruct
    return pl.pallas_call(
        functools.partial(feed_kernel, NZ),
        out_shape=[
            shape((R, D), BF16),
            shape((R, D), F32),
            shape((NZ, R, C), BF16),
            shape((D, NZ * FH), BF16),
            shape((NZ, FH, D), BF16),
            shape((NZ, C, D), BF16),
            shape((16, D), F32),
        ],
        in_specs=[VMEM, VMEM, VMEM, VMEM, ANY, ANY, ANY],
        out_specs=[VMEM, VMEM, VMEM, ANY, ANY, ANY, VMEM],
        scratch_shapes=[
            pltpu.VMEM((D, NZ * FH), BF16),
            pltpu.VMEM((NZ, FH, D), BF16),
            pltpu.VMEM((D, D), BF16),
            pltpu.VMEM((2 * R, D), BF16),
            pltpu.VMEM((2 * R, NZ * FH), BF16),
            pltpu.VMEM((2 * R, NZ * FH), BF16),
            pltpu.VMEM((2 * R, D), BF16),
            pltpu.VMEM((2 * R, NZ * FH), BF16),
            pltpu.VMEM((2, R, D), BF16),
            pltpu.VMEM((R, D), BF16),
            pltpu.VMEM((R, D), BF16),
            pltpu.VMEM((R, D), F32),
            pltpu.VMEM((R, D), F32),
            pltpu.VMEM((R, D), F32),
            pltpu.VMEM((D, NZ * FH), BF16),
            pltpu.VMEM((NZ, FH, D), BF16),
            pltpu.VMEM((NZ, C, D), BF16),
            DMA((3,)),
            DMA((4,)),
            DMA((4,)),
            DMA((3,)),
        ],
        compiler_params=pltpu.CompilerParams(
            collective_id=1, has_side_effects=True, vmem_limit_bytes=58 * 2**20
        ),
    )(inputs, cotangent, o4, par, wa, wb, wo)


def reduce_kernel(
    NZ,
    x_ref,
    dmid_ref,
    par_ref,
    small_in,
    do4_ref,
    wq_ref,
    q_ref,
    k_ref,
    v_ref,
    h1_hbm,
    p_hbm,
    ga_hbm,
    gb_hbm,
    go_hbm,
    dx_ref,
    gb_out,
    ga_out,
    go_out,
    gq_out,
    small_out,
    h1,
    p_s,
    ga,
    gb,
    go_s,
    go_far,
    go_w,
    gq_s,
    gq_far,
    gq_w,
    r1_b,
    r1_a,
    r1_o,
    r1_q,
    r2_b,
    r2_a,
    r2_o,
    r2_q,
    rz_b,
    rz_a,
    rz_o,
    f_b,
    f_a,
    f_o,
    f_q,
    do_all,
    do_st,
    q_st,
    ds_s,
    dq_f,
    dk_f,
    dv_f,
    dqkv,
    dh,
    rel,
    acc,
    s_f,
    s_b,
    s_z,
    s_p,
    s_g,
    load_sem,
    p_sem,
    do_s,
    do_r,
    pair_s,
    pair_r,
    s1_s,
    s1_r,
    s2_s,
    s2_r,
    z_s,
    z_r,
    g_s,
    g_r,
    sib_s,
    sib_r,
    ru_s,
    ru_r,
    rd_s,
    rd_r,
    sz_s,
    sz_r,
    sp_s,
    sp_r,
    out_sem,
):
    R, D = x_ref.shape
    C = D // NZ
    T = NZ * R
    FH = gb.shape[1]
    w, z, core, x, y = place()
    near = {j: flips(w, core, x, y, j) for j in range(1, GROUP)}
    zto = [lax.rem(z + j, NZ) for j in range(NZ)]
    zfrom = [lax.rem(z + NZ - j, NZ) for j in range(NZ)]
    hops = range(1, NZ)
    pending = []

    def go(copy):
        copy.start()
        pending.append(copy)

    loads = [
        pltpu.make_async_copy(src, dst, load_sem.at[i])
        for i, (src, dst) in enumerate(((gb_hbm, gb), (ga_hbm, ga), (go_hbm, go_s), (h1_hbm, h1)))
    ]
    for copy in loads:
        copy.start()
    spans = widths(R, NZ)

    def load_p(b):
        span = pl.ds(0, spans[b])
        return pltpu.make_async_copy(
            p_hbm.at[b, :, span], p_s.at[b % 2, :, span], p_sem.at[b % 2]
        )

    load_p(0).start()
    load_p(1).start()

    meet([(w, zto[j]) for j in hops] + [(near[j], z) for j in range(1, GROUP)])

    first = (x, y)
    second = (y, x)
    flip_first = (2, 4)
    flip_second = (4, 2)
    half = (FH // 4, C // 2, C // 4, C // 4)
    r1 = (r1_b, r1_a, r1_o, r1_q)
    r2 = (r2_b, r2_a, r2_o, r2_q)
    rz = (rz_b, rz_a, rz_o)
    final = (f_b, f_a, f_o, f_q)
    out = (gb_out, ga_out, go_out, gq_out)
    work = (gb, ga, go_w, gq_w)

    def index(kind, part, start, n):
        if kind == 0:
            return at(part * (FH // 2) + start, n), slice(None)
        width = work[kind].shape[2] // 2
        return at(start, n), pl.ds(part * width, width)

    def sub(kind, part, start, n):
        return work[kind].at[(slice(None),) + index(kind, part, start, n)]

    def kept(kind, part):
        return half[kind] * first[part] + (half[kind] // 2) * second[part]

    def step_one(kind, part):
        n = half[kind]
        return remote(
            sub(kind, part, n * (1 - first[part]), n),
            r1[kind].at[part],
            s1_s.at[kind, part],
            s1_r.at[kind, part],
            (near[flip_first[part]], z),
        )

    def step_two(kind, part):
        n = half[kind] // 2
        return remote(
            sub(kind, part, 2 * n * first[part] + n * (1 - second[part]), n),
            r2[kind].at[part],
            s2_s.at[kind, part],
            s2_r.at[kind, part],
            (near[flip_second[part]], z),
        )

    def add_one(kind):
        n = half[kind]
        for part in range(2):
            step_one(kind, part).wait_recv()
            idx = index(kind, part, n * first[part], n)

            @pl.loop(0, NZ)
            def _(d):
                work[kind][(d,) + idx] += r1[kind][part, d]

            go(step_two(kind, part))

    def add_two(kind):
        n = half[kind] // 2
        for part in range(2):
            step_two(kind, part).wait_recv()
            idx = index(kind, part, kept(kind, part), n)

            @pl.loop(0, NZ)
            def _(d):
                work[kind][(d,) + idx] += r2[kind][part, d]

            for j in hops:
                go(along(kind, part, j))

    def along(kind, part, j):
        n = half[kind] // 2
        idx = index(kind, part, kept(kind, part), n)
        target = rz[kind].at[part, j - 1] if kind < 3 else f_q.at[(z,) + idx]
        return remote(
            work[kind].at[(zto[j],) + idx],
            target,
            z_s.at[kind, part, j],
            z_r.at[kind, part, j],
            (w, zto[j]),
        )

    def add_line(kind):
        n = half[kind] // 2
        for part in range(2):
            idx = index(kind, part, kept(kind, part), n)
            for j in hops:
                along(kind, part, j).wait_recv()
            if kind < 3:
                total = work[kind][(z,) + idx].astype(F32)
                for j in hops:
                    total += rz[kind][part, j - 1].astype(F32)
                final[kind][idx] = total.astype(BF16)
            else:
                f_q[(z,) + idx] = work[kind][(z,) + idx]
            for t in range(1, 4):
                go(share(kind, part, t))

    def share(kind, part, t):
        n = half[kind] // 2
        idx = index(kind, part, kept(kind, part), n)
        if kind == 3:
            idx = (slice(None),) + idx
        ref = final[kind].at[idx]
        return remote(
            ref, ref, g_s.at[kind, part, t], g_r.at[kind, part, t], (near[2 * t], z)
        )

    outs = []

    def shared(kind):
        n = half[kind] // 2
        for part in range(2):
            for t in range(1, 4):
                ox = x + (t & 1) * (1 - 2 * x)
                oy = y + (t >> 1) * (1 - 2 * y)
                a, b = (ox, oy) if part == 0 else (oy, ox)
                idx = index(kind, part, half[kind] * a + n * b, n)
                if kind == 3:
                    idx = (slice(None),) + idx
                ref = final[kind].at[idx]
                remote(
                    ref, ref, g_s.at[kind, part, t], g_r.at[kind, part, t], (near[2 * t], z)
                ).wait_recv()
        go(
            remote(
                final[kind], out[kind].at[core], sib_s.at[kind], sib_r.at[kind], (near[1], z)
            )
        )
        copy = pltpu.make_async_copy(final[kind], out[kind].at[core], out_sem.at[kind])
        copy.start()
        outs.append(copy)

    loads[0].wait()
    for part in range(2):
        go(step_one(0, part))
    for j in hops:
        go(
            remote(
                do4_ref.at[zto[j]],
                do_all.at[at(z * R, R)],
                do_s.at[j],
                do_r.at[j],
                (w, zto[j]),
            )
        )
    loads[1].wait()
    for part in range(2):
        go(step_one(1, part))
    loads[2].wait()
    CH = C // 2
    pair_o = remote(
        go_s.at[:, at((1 - core) * CH, CH)], go_far, pair_s.at[0], pair_r.at[0], (near[1], z)
    )
    go(pair_o)
    do_all[at(z * R, R), :] = do4_ref[z]
    dk_f[...] = jnp.zeros_like(dk_f)
    dv_f[...] = jnp.zeros_like(dv_f)
    pair_o.wait_recv()

    @pl.loop(0, NZ)
    def _(d):
        go_w[d] = go_s[d, at(core * CH, CH), :] + go_far[d]

    for part in range(2):
        go(step_one(2, part))
    for j in hops:
        remote(
            do4_ref.at[zto[j]],
            do_all.at[at(zfrom[j] * R, R)],
            do_s.at[j],
            do_r.at[j],
            (w, zto[j]),
        ).wait_recv()

    for b, width in enumerate(spans):
        load_p(b).wait()
        block = slice(b * R, (b + 1) * R)
        slot = b % 2
        dq_f[...] = jnp.zeros_like(dq_f)

        @pl.loop(0, 4)
        def _(h):
            pick = lanes(R, C, h)
            rows = at(h * R, R)
            do_h = do_all[block, :] * pick.astype(BF16)
            do_st[rows, :] = do_h
            q_st[rows, :] = q_ref[block, :] * pick.astype(BF16)
            p = p_s[slot, rows, :width].astype(F32)
            t = p * dot_nt(do_h, v_ref[:width, :])
            ds = (t - p * jnp.sum(t, -1, keepdims=True)).astype(BF16)
            ds_s[rows, :width] = ds
            dq_f[...] += dot(ds, k_ref[:width, :]) * pick

        @pl.loop(0, width // 128)
        def _(n):
            keys = at(n * 128, 128, 128)
            dv_f[keys, :] += dot_tn(p_s[slot, :, keys], do_st[...])
            dk_f[keys, :] += dot_tn(ds_s[:, keys], q_st[...])

        if b + 2 < NZ:
            load_p(b + 2).start()
        dqkv[block, 0:C] = (dq_f[...] * 0.125).astype(BF16)
        if b == NZ - 2:
            add_one(0)
    dqkv[:, C : 2 * C] = (dk_f[:T, :] * 0.125).astype(BF16)
    dqkv[:, 2 * C :] = dv_f[:T, :].astype(BF16)

    for d in range(NZ):
        dh[d] = dot_nt(dqkv[d * R : (d + 1) * R, :], wq_ref[...]).astype(BF16)

    def rise(d):
        return remote(
            dh.at[d], rel.at[d], ru_s.at[d], ru_r.at[d], (w, jnp.minimum(z + 1, NZ - 1))
        )

    def fall(d, last):
        return remote(
            dh.at[d], rel.at[NZ if last else d], rd_s.at[d], rd_r.at[d], (w, jnp.maximum(z - 1, 0))
        )

    def up_step(here, d):
        if here > 0:
            rise(d).wait_recv()
            dh[d] += rel[d]
        rise(d).start()

    def down_step(here, d):
        if here < NZ - 1:
            fall(d, False).wait_recv()
            dh[d] += rel[d]
        fall(d, here - 1 == d).start()

    def actions(here):
        ups = [(up_step, d) for d in range(NZ - 1, here, -1)]
        downs = [(down_step, d) for d in range(here)]
        return ups + downs if here < NZ // 2 else downs + ups

    def line_step(k):
        for here in range(NZ):
            act, d = actions(here)[k]

            @pl.when(z == here)
            def _():
                act(here, d)

    line_step(0)

    loads[3].wait()
    for d in range(NZ):
        gq_s[d] = dot_tn(h1[:, d * C : (d + 1) * C], dqkv[...]).astype(BF16)
    pair_q = remote(
        gq_s.at[:, at((1 - core) * CH, CH)], gq_far, pair_s.at[1], pair_r.at[1], (near[1], z)
    )
    go(pair_q)
    for d in range(NZ):
        s_f[d] = small_in[:, d * C : (d + 1) * C]
    s_f[z, 8:9, :] = rowsum(dqkv[:, 0:C].astype(F32))
    s_f[z, 9:10, :] = rowsum(dqkv[:, 2 * C :].astype(F32))
    add_one(1)
    pair_q.wait_recv()

    @pl.loop(0, NZ)
    def _(d):
        gq_w[d] = gq_s[d, at(core * CH, CH), :] + gq_far[d]

    for part in range(2):
        go(step_one(3, part))
    line_step(1)
    add_one(2)
    add_two(0)
    line_step(2)
    add_one(3)
    add_two(1)
    add_two(2)
    add_two(3)

    acc[...] = dh[z].astype(F32)

    @pl.when(z > 0)
    def _():
        remote(
            dh.at[z], rel.at[z], ru_s.at[z], ru_r.at[z], (w, jnp.minimum(z + 1, NZ - 1))
        ).wait_recv()
        acc[...] += rel[z].astype(F32)

    @pl.when(z < NZ - 1)
    def _():
        remote(
            dh.at[z], rel.at[NZ], rd_s.at[z], rd_r.at[z], (w, jnp.maximum(z - 1, 0))
        ).wait_recv()
        acc[...] += rel[NZ].astype(F32)

    dh1 = acc[...]
    n1, inverse = norm(x_ref[...].astype(F32))
    dx_ref[...] = (dmid_ref[...] + norm_back(dh1, n1, inverse, par_ref[0:1, :])).astype(BF16)
    gain = rowsum(dh1 * n1)
    shift = rowsum(dh1)
    for d in range(NZ):
        s_f[d, 0:1, :] = gain[:, d * C : (d + 1) * C]
        s_f[d, 4:5, :] = shift[:, d * C : (d + 1) * C]
    s_b[...] = s_f[...].astype(BF16)
    for j in hops:
        go(remote(s_b.at[zto[j]], s_z.at[j], sz_s.at[j], sz_r.at[j], (w, zto[j])))
    for j in hops:
        remote(s_b.at[zto[j]], s_z.at[j], sz_s.at[j], sz_r.at[j], (w, zto[j])).wait_recv()
    total = s_f[z]
    for j in hops:
        total += s_z[j].astype(F32)
    s_p[...] = total.astype(BF16)
    for j in range(1, GROUP):
        go(remote(s_p, s_g.at[j], sp_s.at[j], sp_r.at[j], (near[j], z)))

    for kind in range(4):
        add_line(kind)
    for j in range(1, GROUP):
        remote(s_p, s_g.at[j], sp_s.at[j], sp_r.at[j], (near[j], z)).wait_recv()
        total += s_g[j].astype(F32)
    small_out[...] = total
    for kind in range(4):
        shared(kind)
    for kind in range(4):
        remote(
            final[kind], out[kind].at[1 - core], sib_s.at[kind], sib_r.at[kind], (near[1], z)
        ).wait_recv()
    for here in range(NZ):

        @pl.when(z == here)
        def _():
            for act, d in actions(here):
                if act is up_step:
                    rise(d).wait_send()
                else:
                    fall(d, here - 1 == d).wait_send()

    for copy in pending:
        copy.wait_send()
    for copy in outs:
        copy.wait()


def reduce(NZ, inputs, dmid, par, small, do4, wq, q, k, v, h1, p, ga, gb, go):
    R, D = inputs.shape
    C = D // NZ
    T = NZ * R
    FH = gb.shape[1]
    wide = p.shape[2]
    F = NZ * FH
    shape = jax.ShapeDtypeStruct
    buf = pltpu.VMEM
    return pl.pallas_call(
        functools.partial(reduce_kernel, NZ),
        out_shape=[
            shape((R, D), BF16),
            shape((2, FH, D), BF16),
            shape((2, C, F), BF16),
            shape((2, C // 2, D), BF16),
            shape((2, NZ, C // 2, 3 * C), BF16),
            shape((16, C), F32),
        ],
        in_specs=[VMEM] * 9 + [ANY] * 5,
        out_specs=[VMEM, ANY, ANY, ANY, ANY, VMEM],
        scratch_shapes=[
            buf((T, D), BF16),
            buf((2, 4 * R, wide), BF16),
            buf((NZ, C, F), BF16),
            buf((NZ, FH, D), BF16),
            buf((NZ, C, D), BF16),
            buf((NZ, C // 2, D), BF16),
            buf((NZ, C // 2, D), BF16),
            buf((NZ, C, 3 * C), BF16),
            buf((NZ, C // 2, 3 * C), BF16),
            buf((NZ, C // 2, 3 * C), BF16),
            buf((2, NZ, FH // 4, D), BF16),
            buf((2, NZ, C // 2, F // 2), BF16),
            buf((2, NZ, C // 4, D // 2), BF16),
            buf((2, NZ, C // 4, 3 * C // 2), BF16),
            buf((2, NZ, FH // 8, D), BF16),
            buf((2, NZ, C // 4, F // 2), BF16),
            buf((2, NZ, C // 8, D // 2), BF16),
            buf((2, NZ, C // 8, 3 * C // 2), BF16),
            buf((2, NZ - 1, FH // 8, D), BF16),
            buf((2, NZ - 1, C // 4, F // 2), BF16),
            buf((2, NZ - 1, C // 8, D // 2), BF16),
            buf((FH, D), BF16),
            buf((C, F), BF16),
            buf((C // 2, D), BF16),
            buf((NZ, C // 2, 3 * C), BF16),
            buf((T, C), BF16),
            buf((4 * R, C), BF16),
            buf((4 * R, C), BF16),
            buf((4 * R, wide), BF16),
            buf((R, C), F32),
            buf((wide, C), F32),
            buf((wide, C), F32),
            buf((T, 3 * C), BF16),
            buf((NZ, R, D), BF16),
            buf((NZ + 1, R, D), BF16),
            buf((R, D), F32),
            buf((NZ, 16, C), F32),
            buf((NZ, 16, C), BF16),
            buf((NZ, 16, C), BF16),
            buf((16, C), BF16),
            buf((GROUP, 16, C), BF16),
            DMA((4,)),
            DMA((2,)),
            DMA((NZ,)),
            DMA((NZ,)),
            DMA((2,)),
            DMA((2,)),
            DMA((4, 2)),
            DMA((4, 2)),
            DMA((4, 2)),
            DMA((4, 2)),
            DMA((4, 2, NZ)),
            DMA((4, 2, NZ)),
            DMA((4, 2, 4)),
            DMA((4, 2, 4)),
            DMA((4,)),
            DMA((4,)),
            DMA((NZ,)),
            DMA((NZ,)),
            DMA((NZ,)),
            DMA((NZ,)),
            DMA((NZ,)),
            DMA((NZ,)),
            DMA((GROUP,)),
            DMA((GROUP,)),
            DMA((4,)),
        ],
        compiler_params=pltpu.CompilerParams(
            collective_id=2, has_side_effects=True, vmem_limit_bytes=60 * 2**20
        ),
    )(inputs, dmid, par, small, do4, wq, q, k, v, h1, p, ga, gb, go)


def shards(NZ, W, inputs, w_qkv, w_out, w_fc1, w_fc2, norm_gain, shifts, text_len, cotangent):
    R, D = inputs.shape[1:]
    C = D // NZ
    FF = w_fc1.shape[1]
    FH = FF // (2 * NZ)
    par = jnp.concatenate([norm_gain, shifts], 0)
    o4, h1, q, k, v, wq, wa, wb, wo, par_f, p = attend(
        NZ, inputs[0], par, text_len, w_qkv, w_out, w_fc1, w_fc2
    )
    act, dmid, do4, ga, gb, go, small = feed(NZ, inputs[0], cotangent[0], o4, par_f, wa, wb, wo)
    ga = ga.reshape(NZ, C, NZ * FH)
    dx, gb, ga, go, gq, small = reduce(
        NZ, inputs[0], dmid, par_f, small, do4, wq, q, k, v, h1, p, ga, gb, go
    )
    grads = (
        gq.reshape(2, NZ, C // 2, 3, C).transpose(0, 2, 3, 1, 4).reshape(C, 3 * D).astype(F32),
        go.reshape(C, D).astype(F32),
        ga.reshape(2, C, NZ, FH).transpose(1, 2, 0, 3).reshape(C, FF).astype(F32),
        gb.reshape(2 * FH, D).astype(F32),
        small,
    )
    if W > GROUP:
        groups = [list(range(i, W, GROUP)) for i in range(GROUP)]
        grads = lax.psum(grads, "wide", axis_index_groups=groups)
    return (act[None], dx[None]) + tuple(grads[:4]) + (grads[4][:4], grads[4][4:])


def solution(mesh):
    return jax.shard_map(
        functools.partial(shards, mesh.shape["narrow"], mesh.shape["wide"]),
        mesh=mesh,
        in_specs=(
            P("wide", "narrow", None),
            P("narrow", None),
            P("narrow", None),
            P("narrow", None),
            P("narrow", None),
            P(None, "narrow"),
            P(None, "narrow"),
            P("wide"),
            P("wide", "narrow", None),
        ),
        out_specs=(
            P("wide", "narrow", None),
            P("wide", "narrow", None),
            P("narrow", None),
            P("narrow", None),
            P("narrow", None),
            P("narrow", None),
            P(None, "narrow"),
            P(None, "narrow"),
        ),
        check_vma=False,
    )
```

time: 1500 us -> 415 us (0.28)
  waiting for transfers between devices: 925 us -> 0 us
  Pallas kernels: 0 us -> 368 us
  blocking collectives: 279 us -> 0 us
  matrix products: 201 us -> 0 us
  local copies, waits for them, and re-layouts: 55.5 us -> 32.8 us
    all_gather x6 -> x0, waiting for transfers between devices: 480 us -> none  [the longest x1 145 us: shards(): lax.all_gather(w_fc1, 'narrow', axis=0, tiled=True)]
    reduce_scatter x5 -> x0, waiting for transfers between devices: 426 us -> none  [the longest x1 148 us: shards(): lax.psum_scatter(grad_fc1_term.astype(jnp.bfloat16), 'narrow', scatter_di...]
    pallas_call x0 -> x3, Pallas kernels: none -> 368 us  [the longest x1 190 us: reduce(): pl.pallas_call(functools.partial(reduce_kernel, NZ), out_shape=[shape((R,...]
    psum x1 -> x0, blocking collectives: 250 us -> none  [shards(): lax.psum((pieces[0], pieces[1], pieces[2], pieces[3], pieces[4], pieces[5...]
    dot_general x17 -> x0, matrix products: 188 us -> none  [the longest x1 42.3 us: shards(): jnp.einsum('hqk,qhe->khe', d_raw, queries.reshape(local_rows, head_count,...]
    unnamed x85 -> x10, local copies, waits for them, and re-layouts: 44.3 us -> 1.62 us
    all_gather x2 -> x0, blocking collectives: 28.7 us -> none  [the longest x1 15 us: shards(): lax.all_gather(shifts, 'narrow', axis=1, tiled=True)]
    convert_element_type x2 -> x6, local copies, waits for them, and re-layouts: 1.76 us -> 28.6 us  [the longest x3 18.6 us: shards(): ga.reshape(2, C, NZ, FH).transpose(1, 2, 0, 3).reshape(C, FF).astype(F32)]
  transfers between devices with their start and end apart: 14 -> 0, of which waited for: 11 -> 0; matrix products, arithmetic and copies ran while one was open for 14% -> 0% of each run, Pallas kernels for 0% -> 0%
where the time goes in v1:
time: 415 us; the launch traced here: 409 us
  Pallas kernels  368 us (89%)
  local copies, waits for them, and re-layouts  32.8 us (8%)
  other arithmetic  6.04 us (1%)
    pallas_call x1, Pallas kernels, reduce(): pl.pallas_call(functools.partial(reduce_kernel, NZ), out_shape=[shape((R,...  190 us
    pallas_call x1, Pallas kernels, attend(): pl.pallas_call(functools.partial(attend_kernel, NZ), out_shape=[shape((NZ...  148 us
    pallas_call x1, Pallas kernels, feed(): pl.pallas_call(functools.partial(feed_kernel, NZ), out_shape=[shape((R, D...  30.9 us
    convert_element_type x3, local copies, waits for them, and re-layouts, shards(): ga.reshape(2, C, NZ, FH).transpose(1, 2, 0, 3).reshape(C, FF).astype(F32)  18.6 us
    convert_element_type x3, local copies, waits for them, and re-layouts, shards(): gq.reshape(2, NZ, C // 2, 3, C).transpose(0, 2, 3, 1, 4).reshape(C, 3 * D)  9.96 us

profile of v1, /device:TPU:0, one launch (start us, length us, event | category | flops | bytes accessed | tf_op | source)
XLA Modules:
  0.0 408.9 jit_solution(13451998032600277920)
XLA Ops:
  1.3 1.3 pad_maximum_fusion.par_ref
  2.6 147.9 %shard_map.152 = (bf16[4,272,256]{2,1,0:T(8,128)(2,1)}, bf16[1088,1024]{1,0:T(8,128)(2,1)}, bf16[1088,256]{1,0:T(8,128)(2,1)}, bf16[1152,256]{1,0:T(8,128)(2,1)}...) custom-call(bf16[272,1024]{1,0:T(8,128)(2,1)} %bitcast.17, ...), custom_call_target="tpu_custom_call" | custom-call | tf_op jit(solution)/shard_map/pallas_call | solution.py:459
  150.5 30.9 %shard_map.153 = (bf16[272,1024]{1,0:T(8,128)(2,1)}, f32[272,1024]{1,0:T(8,128)}, bf16[4,272,256]{2,1,0:T(8,128)(2,1)}, bf16[1024,2048]{1,0:T(8,128)(2,1)}, bf16...) custom-call(bf16[272,1024]{1,0:T(8,128)(2,1)} %bitcast.18, ...), custom_call_target="tpu_custom_call" | custom-call | tf_op jit(solution)/shard_map/pallas_call | solution.py:698
  181.4 189.7 %shard_map.154 = (bf16[272,1024]{1,0:T(8,128)(2,1)}, bf16[2,512,1024]{2,1,0:T(8,128)(2,1)}, bf16[2,256,2048]{2,1,0:T(8,128)(2,1)}, bf16[2,128,1024]{2,1,0:T(8,12...) custom-call(bf16[272,1024]{1,0:T(8,128)(2,1)} %bitcast.19, f32[272,1024]{1,0:T(8,128)} %get-tuple-element.38.dmid_ref, ...), custom_call_target="tpu_custom_call" | custom-call | tf_op jit(solution)/shard_map/pallas_call | solution.py:1212
  371.1 1.3 slice.6
  372.4 1.3 slice.7
  373.7 2.1 bitcast_convert_fusion.1
  375.8 1.9 copy.21
  377.8 2.8 copy.22
  380.5 0.0 copy-start.1
  380.5 5.3 %reshape.38 = f32[256,3072]{1,0:T(8,128)} reshape(f32[2,128,3,4,256]{4,3,2,1,0:T(4,128)} %copy.22) | data formatting | bytes 6291456 | tf_op jit(solution)/shard_map/convert_element_type | solution.py:1313
  385.8 0.0 copy-done.1
  385.8 4.5 %reshape.43 = f32[2,256,4,512]{3,2,1,0:T(4,128)} reshape(bf16[2,256,2048]{2,1,0:T(8,128)(2,1)S(1)} %copy-done.1) | data formatting | bytes 6291456 | tf_op jit(solution)/shard_map/convert_element_type | solution.py:1315
  390.3 7.4 %copy.23 = f32[256,4,2,512]{3,2,1,0:T(2,128)} copy(f32[256,4,2,512]{3,1,0,2:T(4,128)} %bitcast.15) | data formatting | bytes 8388608 | tf_op jit(solution)/shard_map/convert_element_type | solution.py:1315
  397.7 0.0 copy-start
  397.7 6.8 %reshape.40 = f32[256,4096]{1,0:T(8,128)} reshape(f32[256,4,2,512]{3,2,1,0:T(2,128)} %copy.23) | data formatting | bytes 8388608 | tf_op jit(solution)/shard_map/convert_element_type | solution.py:1315
  404.4 0.0 copy-done
  404.4 0.0 copy-start.2
  404.4 0.0 copy-start.3
  404.4 2.6 bitcast_convert_fusion
  407.0 0.0 copy-done.2
  407.0 0.8 copy.27
  407.8 0.0 copy-done.3
  407.8 0.8 copy.28
Async XLA Ops:
  380.5 5.3 %copy-start.1 = (bf16[2,256,2048]{2,1,0:T(8,128)(2,1)S(1)}, bf16[2,256,2048]{2,1,0:T(8,128)(2,1)}, u32[]{:S(2)}) copy-start(bf16[2,256,2048]{2,1,0:T(8,128)(2,1)} %get-tuple-element.53) | copy-start | bytes 6291460
  397.7 6.8 %copy-start = (bf16[2,512,1024]{2,1,0:T(8,128)(2,1)S(1)}, bf16[2,512,1024]{2,1,0:T(8,128)(2,1)}, u32[]{:S(2)}) copy-start(bf16[2,512,1024]{2,1,0:T(8,128)(2,1)} %get-tuple-element.54) | copy-start | bytes 6291460
  404.4 2.6 copy-start.2
  404.4 3.4 copy-start.3
